TPU v7x, 128 devices: a whole 4x4x4 slice. The times are simulated.
128 devices in a mesh: member: 16 (over z, y_lo, core), band: 8 (over x, y_hi).
Axes of the slice: x: 4, y: 4 (y_hi: 2, y_lo: 2; y = y_hi * 2 + y_lo), z: 4, core: 2. Of those that a mesh axis runs over, the one named last changes fastest.
Arguments:
- states: bfloat16 [32, 84, 128, 128], P('member', None, 'band'), may hold values from -6 to 6
- noise_field: float32 [32, 84, 128, 128], P('member', None, 'band'), may hold values from -3 to 3
- target: bfloat16 [84, 128, 128], P(None, 'band'), may hold values from -6 to 6
- w_conv: bfloat16 [512, 756], replicated, may hold values from -0.21875 to 0.21875
- w_proj: bfloat16 [84, 512], replicated, may hold values from -0.25 to 0.25
- matchings: int32 [4, 32], replicated, may hold values from 0 to 31, each once within a row
Outputs:
- grad_states: bfloat16 [32, 84, 128, 128], P('member', None, 'band')
- grad_conv: float32 [512, 756], P(('member', 'band'))
- grad_proj: float32 [84, 512], P(None, ('member', 'band'))
Inputs may be any that keep to these rules, and one draw needn't show every extreme that they name: `matchings`: each row is a permutation of the 32 member numbers.
All inputs are finite; a program needn't handle non-finite values.
Results may differ from a plain program's by a relative error of at most 0.0075.
Values may be sent and summed in bfloat16 or wider, within the bound.
A program may use at most 128 MiB of HBM per device.

v0:
```python
import functools

import jax
import jax.numpy as jnp
import ml_dtypes
import numpy as np
from jax import lax
from jax.experimental import pallas as pl
from jax.experimental.pallas import tpu as pltpu
from jax.sharding import PartitionSpec as P

F32, BF16 = jnp.float32, jnp.bfloat16
MESH = pl.DeviceIdType.MESH
V, VP, VQ = 84, 96, 88
VH = VP // 2
R, C, H = 16, 128, 512
NM, NB, NK = 16, 8, 4
GROUP = NM // 2 * NB
MEMBERS = 2 * NM
KP = 256
CHUNKS = (384, 256, 256)


def patch_order():
    table = np.zeros((8, 8 * C, C), ml_dtypes.bfloat16)
    for row in range(8):
        for lon in range(C):
            group, patch, col = lon // 8, lon % 8 // 4, lon % 4
            table[group // 2, row * C + lon, group % 2 * 64 + (row * 4 + col) * 2 + patch] = 1
    return table


def remote(src, dst, send_sem, recv_sem, **device):
    return pltpu.make_async_remote_copy(
        src_ref=src, dst_ref=dst, send_sem=send_sem, recv_sem=recv_sem,
        device_id=device, device_id_type=MESH,
    )


def gelu_and_slope(x):
    phi = 0.5 + 0.5 * lax.erf(x * 0.7071067811865476)
    bell = jnp.exp2((x * x) * (-0.5 * 1.4426950408889634) - 1.3257480647361593)
    return x * phi, phi + x * bell


def dot(a, b):
    return jnp.dot(a, b, preferred_element_type=F32)


def dot_nt(a, b):
    return lax.dot_general(a, b, (((1,), (1,)), ((), ())), preferred_element_type=F32)


def kernel(
    states_in, noise_in, target_in, w_conv_in, w_proj_in, perm_in, match, match_v,
    out, sums,
    states, noise, target, w_conv, w_proj, perm, inverse_v, inverse, wide_w, load,
    xf, x3, hs, hb, wf, wt, wp, wpt, hidden, slope, pn, sb, rb, pf, tf, tp, es, sc, gb, gr, gn, gp, of,
    hsb, hrb, a0, a1, a2, s10, s11, s12, r10, r11, r12, s3, r3,
    h_send, h_recv, p_send, p_recv, g_send, g_recv, o_send, o_recv,
    u_send, u_recv, w_send, w_recv, ready,
):
    me, band = lax.axis_index("member"), lax.axis_index("band")
    core, chip = lax.rem(me, 2), lax.div(me, 2)
    lanes = lax.broadcasted_iota(jnp.int32, (VP, C), 1)
    acc = (a0, a1, a2)
    s1, r1 = (s10, s11, s12), (r10, r11, r12)
    spot = chip * NB + band

    halves = lax.broadcasted_iota(jnp.int32, (VH, C), 1) < 64
    loads = [
        pltpu.make_async_copy(a, b, load.at[k])
        for k, (a, b) in enumerate((
            (w_conv_in, w_conv), (w_proj_in, w_proj), (noise_in, noise), (states_in, states),
            (target_in, target), (perm_in, perm),
        ))
    ]
    for copy in loads:
        copy.start()
    barrier = pltpu.get_barrier_semaphore()

    def greet_member(step, _):
        pl.semaphore_signal(barrier, inc=1, device_id={"member": lax.rem(me + step, NM)}, device_id_type=MESH)
        return 0

    def greet_band(step, _):
        pl.semaphore_signal(barrier, inc=1, device_id={"band": lax.rem(band + step, NB)}, device_id_type=MESH)
        return 0

    lax.fori_loop(1, NM, greet_member, 0)
    lax.fori_loop(1, NB, greet_band, 0)

    to_member = lax.broadcasted_iota(jnp.int32, (MEMBERS, MEMBERS), 0)
    number = lax.broadcasted_iota(jnp.int32, (MEMBERS, MEMBERS), 1)
    column = lax.broadcasted_iota(jnp.int32, (MEMBERS, C), 1)
    table = jnp.zeros((MEMBERS, C), jnp.int32)
    for k in range(NK):
        hit = jnp.where(match_v[k:k + 1, :] == to_member, number, 0)
        table = jnp.where(column == k, jnp.max(hit, axis=1, keepdims=True), table)
    inverse_v[...] = table
    to_scalars = pltpu.make_async_copy(inverse_v, inverse, load.at[6])
    to_scalars.start()

    for copy in loads[:2]:
        copy.wait()
    wide_w[...] = w_conv[...].astype(F32)
    for ro in range(3):
        base = ro * 3 * V
        parts = [wide_w[base + co * V:base + co * V + 80, :] for co in range(3)]
        parts += [wide_w[base + co * V + 80:base + (co + 1) * V, :] for co in range(3)]
        w_part = jnp.concatenate(parts + [jnp.zeros((KP - 3 * V, H), F32)], axis=0)
        wt[:, ro * H:(ro + 1) * H] = w_part.astype(BF16)
        wf[:, ro * KP:(ro + 1) * KP] = w_part.T.astype(BF16)
    w_pad = jnp.concatenate([w_proj[...].astype(F32), jnp.zeros((VP - V, H), F32)], axis=0)
    wp[...] = w_pad.astype(BF16)
    wpt[...] = w_pad.T.astype(BF16)

    for copy in loads[2:5]:
        copy.wait()
    def add_inputs(c, _):
        part = pl.ds(c * 12, 12)
        to = pl.ds(pl.multiple_of(c * 192, 192), 192)
        for m in range(2):
            value = (states[m, part].astype(F32) + noise[m, part]).astype(BF16).astype(F32)
            xf[m, to, :] = value.reshape(192, C)
        tf[to, :] = target[part].astype(F32).reshape(192, C)
        return 0

    lax.fori_loop(0, V // 12, add_inputs, 0)
    for m in range(2):
        xf[m, V * R:, :] = jnp.zeros(((VP - V) * R, C), F32)
    tf[V * R:, :] = jnp.zeros(((VP - V) * R, C), F32)

    for side, row in ((0, 0), (1, R - 1)):
        for m in range(2):
            hs[side, m] = xf[m, pl.ds(row, VP, stride=R), :].astype(BF16)

    def put_row(m, slot, x):
        left = jnp.where(lanes == 0, 0.0, pltpu.roll(x, 1, 1))
        right = jnp.where(lanes == C - 1, 0.0, pltpu.roll(x, C - 1, 1))
        x3[m, slot, 0:80, :] = left[0:80].astype(BF16)
        x3[m, slot, 80:160, :] = x[0:80].astype(BF16)
        x3[m, slot, 160:240, :] = right[0:80].astype(BF16)
        first = left[80:88] + pltpu.roll(x[80:88], 4, 0)
        x3[m, slot, 240:256, :] = jnp.concatenate([first, right[80:88]], axis=0).astype(BF16)

    def build(r, _):
        for m in range(2):
            put_row(m, r + 1, xf[m, pl.ds(r, VP, stride=R), :])
        return 0

    lax.fori_loop(0, R, build, 0)

    loads[5].wait()
    pl.semaphore_wait(barrier, NM + NB - 2)

    def all_here(step, _):
        pl.semaphore_signal(ready, inc=1, device_id={"band": lax.rem(band + step, NB)}, device_id_type=MESH)
        return 0

    lax.fori_loop(1, NB, all_here, 0)
    def halo(side):
        to = band - 1 if side == 0 else band + 1
        return remote(hs.at[side], hb.at[1 - side], h_send.at[side], h_recv.at[1 - side], band=to)

    pl.when(band > 0)(lambda: halo(0).start())
    pl.when(band < NB - 1)(lambda: halo(1).start())

    def halo_in(side, slot):
        remote(hs.at[1 - side], hb.at[side], h_send.at[1 - side], h_recv.at[side], band=band).wait_recv()
        for m in range(2):
            put_row(m, slot, hb[side, m].astype(F32))

    def no_halo(slot):
        for m in range(2):
            x3[m, slot] = jnp.zeros((KP, C), BF16)

    def halo_rows():
        pl.when(band > 0)(lambda: halo_in(0, 0))
        pl.when(band == 0)(lambda: no_halo(0))
        pl.when(band < NB - 1)(lambda: halo_in(1, R + 1))
        pl.when(band == NB - 1)(lambda: no_halo(R + 1))

    def pair(ref, m, i):
        return jnp.concatenate([ref[m, i], ref[m, i + 1]], axis=1)

    def order():
        return jnp.concatenate([perm[t] for t in range(8)], axis=1)

    def half_turn(a):
        return pltpu.roll(a, 64, 1)

    def predicted_copy(pr, j, source):
        return remote(sb.at[pr, j], rb.at[pr, source], p_send.at[pr, j], p_recv.at[pr, source], member=j)

    def forward(rp, _):
        i = rp * 2
        for m in range(2):
            columns = jnp.concatenate([pair(x3, m, i + ro) for ro in range(3)], axis=0)
            for part in range(0, H, H // 2):
                rows = slice(part, part + H // 2)
                value, grad = gelu_and_slope(dot(wf[rows, :], columns))
                value = value.astype(BF16)
                for k in range(2):
                    hidden[m, i + k, rows, :] = value[:, k * C:(k + 1) * C]
                    slope[m, i + k, rows, :] = grad[:, k * C:(k + 1) * C]
        return 0

    def predict(pr):
        for m in range(2):
            for r in range(0, 8, 4):
                i = pr * 8 + r
                more = dot(wp[...], jnp.concatenate([hidden[m, i + k] for k in range(4)], axis=1))
                for k in range(0, 4, 2):
                    own = jnp.concatenate([xf[m, pl.ds(i + k + n, VP, stride=R), :] for n in range(2)], axis=1)
                    pn[(r + k) // 2, m * VP:(m + 1) * VP, :] = (own + more[:, k * C:(k + 2) * C]).astype(BF16)
        moved = dot(jnp.concatenate([pn[rp] for rp in range(4)], axis=1), order())
        for t in range(8):
            for m in range(2):
                low = moved[m * VP:m * VP + VH, t * C:(t + 1) * C]
                high = moved[m * VP + VH:(m + 1) * VP, t * C:(t + 1) * C]
                sb[pr, 2 * t, m] = jnp.where(halves, low, half_turn(high)).astype(BF16)
                sb[pr, 2 * t + 1, m] = jnp.where(halves, half_turn(low), high).astype(BF16)

        def send(step, _):
            j = lax.rem(me + step, NM)
            predicted_copy(pr, j, me).start()
            return 0

        lax.fori_loop(1, NM, send, 0)
        rb[pr, me] = sb[pr, me]

    def truth_patches():
        rows = [
            jnp.concatenate([tf[pl.ds(pr * 8 + r, VP, stride=R), :] for r in range(8)], axis=1)
            for pr in range(2)
        ]
        moved = dot(jnp.concatenate(rows, axis=0).astype(BF16), perm[chip])
        for pr in range(2):
            low, high = moved[pr * VP:pr * VP + VH], moved[pr * VP + VH:(pr + 1) * VP]
            first = jnp.where(halves, low, half_turn(high))
            second = jnp.where(halves, half_turn(low), high)
            tp[pr] = jnp.where(core == 0, first, second)

    def square(d):
        d = d * d
        total = d[0:8]
        for k in range(1, VH // 8):
            total = total + d[k * 8:(k + 1) * 8]
        return total

    def gradient_copy(pr, j, source):
        return remote(gb.at[pr, j], gr.at[pr, source], g_send.at[pr, j], g_recv.at[pr, source], member=j)

    def score(pr):
        def arrive(step, _):
            source = lax.rem(me + step, NM)
            predicted_copy(pr, source, source).wait_recv()
            return 0

        lax.fori_loop(1, NM, arrive, 0)

        def widen(source, _):
            for m in range(2):
                pf[source * 2 + m] = rb[pr, source, m].astype(F32)
            return 0

        lax.fori_loop(0, NM, widen, 0)

        def edges(m, _):
            own = pf[m]
            es[pl.ds(pl.multiple_of((NK * MEMBERS + m) * 8, 8), 8), :] = square(own - tp[pr])
            for k in range(NK):
                es[pl.ds(pl.multiple_of((k * MEMBERS + m) * 8, 8), 8), :] = square(own - pf[match[k, m]])
            return 0

        lax.fori_loop(0, MEMBERS, edges, 0)
        count = (NK + 1) * MEMBERS
        total = es[pl.ds(0, count, stride=8), :]
        for k in range(1, 8):
            total = total + es[pl.ds(k, count, stride=8), :]
        for shift in (2, 4, 8, 16, 32, 64):
            total = total + pltpu.roll(total, shift, 1)
        sc[...] = lax.rsqrt(total / (32.0 * V) + 1e-06)

        def member_grad(j):
            for mm in range(2):
                m = j * 2 + mm
                own = pf[m]
                pairs = jnp.zeros((VH, C), F32)
                for k in range(NK):
                    n, n_inv = match[k, m], inverse[m, k]
                    pairs = pairs + (own - pf[n]) * sc[pl.ds(k * MEMBERS + m, 1), :]
                    pairs = pairs + (own - pf[n_inv]) * sc[pl.ds(k * MEMBERS + n_inv, 1), :]
                truth = (own - tp[pr]) * sc[pl.ds(NK * MEMBERS + m, 1), :]
                gb[pr, j, mm] = (truth - pairs * (0.5 / NK)).astype(BF16)

        def member_pair(step, _):
            j = lax.rem(me + step, NM)
            member_grad(j)
            gradient_copy(pr, j, me).start()
            return 0

        lax.fori_loop(1, NM, member_pair, 0)
        member_grad(me)
        gr[pr, me] = gb[pr, me]

    def back_to_rows(pr):
        def gradients_in(step, _):
            source = lax.rem(me + step, NM)
            gradient_copy(pr, source, source).wait_recv()
            return 0

        lax.fori_loop(1, NM, gradients_in, 0)
        parts = []
        for t in range(8):
            rows = []
            for m in range(2):
                first, second = gr[pr, 2 * t, m].astype(F32), gr[pr, 2 * t + 1, m].astype(F32)
                rows.append(jnp.where(halves, first, half_turn(second)))
                rows.append(jnp.where(halves, half_turn(first), second))
            parts.append(jnp.concatenate(rows, axis=0).astype(BF16))
        back = dot_nt(jnp.concatenate(parts, axis=1), order()).astype(BF16)
        for m in range(2):
            for r in range(8):
                gn[m, pr * 8 + r] = back[m * VP:(m + 1) * VP, r * C:(r + 1) * C]

        def hidden_grad(rp, _):
            i = pr * 8 + rp * 2
            for m in range(2):
                dh = dot(wpt[...], pair(gn, m, i))
                for k in range(2):
                    gp[m, i + k + 1] = (dh[:, k * C:(k + 1) * C] * slope[m, i + k]).astype(BF16)
            return 0

        lax.fori_loop(0, 4, hidden_grad, 0)

    def wide(ref, i):
        return jnp.concatenate([ref[m, i + k] for m in range(2) for k in range(8)], axis=1)

    def conv_term(ro, pr):
        term = dot_nt(wide(gp, pr * 8 + 1), wide(x3, pr * 8 + ro))
        acc[ro][:, 0:KP] = term if pr == 0 else acc[ro][:, 0:KP] + term

    def proj_term(pr):
        term = dot_nt(wide(hidden, pr * 8), wide(gn, pr * 8))
        acc[0][:, KP:KP + VP] = term if pr == 0 else acc[0][:, KP:KP + VP] + term

    def core_copy(q):
        return remote(s1[q], r1[q], u_send.at[q], u_recv.at[q], member=me + 1 - 2 * core)

    def core_send(q):
        for c in range(NM // 2):
            base = c * 64 + (1 - core) * 32
            s1[q][c] = acc[q][pl.ds(pl.multiple_of(base, 32), 32), :].astype(BF16)
        core_copy(q).start()

    def sum_copy(place, source):
        return remote(
            s3.at[place], r3.at[source], w_send.at[place], w_recv.at[source],
            member=2 * lax.div(place, NB) + core, band=lax.rem(place, NB),
        )

    def sum_send():
        for q in range(3):
            core_copy(q).wait_recv()
        top = lax.broadcasted_iota(jnp.int32, (8, C), 0) < 4

        def pack(c, _):
            tiles = []
            for q in range(3):
                rows = pl.ds(pl.multiple_of(c * 64 + core * 32, 32), 32)
                value = acc[q][rows, :] + r1[q][c].astype(F32)
                tiles += [value[:, k * C:(k + 1) * C] for k in range(CHUNKS[q] // C)]
            tiles.append(jnp.zeros((32, C), F32))
            for g in range(4):
                parts = [tile[g * 8:(g + 1) * 8] for tile in tiles]
                turned = [pltpu.roll(part, 4, 0) for part in parts]
                first = [jnp.where(top, parts[k], turned[k + 1]) for k in range(0, 8, 2)]
                second = [jnp.where(top, turned[k], parts[k + 1]) for k in range(0, 8, 2)]
                s3[c * NB + 2 * g] = jnp.concatenate(first, axis=0).astype(BF16)
                s3[c * NB + 2 * g + 1] = jnp.concatenate(second, axis=0).astype(BF16)
            return 0

        lax.fori_loop(0, NM // 2, pack, 0)
        pl.semaphore_wait(ready, NB - 1)

        def send(step, _):
            sum_copy(lax.rem(spot + step, GROUP), spot).start()
            return 0

        lax.fori_loop(1, GROUP, send, 0)

    lax.fori_loop(1, 4, forward, 0)
    truth_patches()
    gp_zero = jnp.zeros((H, C), BF16)
    for m in range(2):
        gp[m, 0] = gp_zero
        gp[m, R + 1] = gp_zero
    acc[0][:, KP:] = jnp.zeros((H, 128), F32)
    halo_rows()
    forward(0, 0)
    predict(0)
    lax.fori_loop(4, 8, forward, 0)
    predict(1)
    to_scalars.wait()
    score(0)
    score(1)
    back_to_rows(0)
    proj_term(0)
    for ro in range(3):
        conv_term(ro, 0)
    back_to_rows(1)
    proj_term(1)
    conv_term(0, 1)
    core_send(0)
    conv_term(1, 1)
    core_send(1)
    conv_term(2, 1)
    core_send(2)

    def fold(d):
        def spread(a):
            return (
                jnp.where(lanes[0:a.shape[0]] == C - 1, 0.0, pltpu.roll(a, C - 1, 1)),
                jnp.where(lanes[0:a.shape[0]] == 0, 0.0, pltpu.roll(a, 1, 1)),
            )
        body = spread(d[0:80])[0] + d[80:160] + spread(d[160:240])[1]
        last = spread(d[240:248])[0] + pltpu.roll(d[240:248], 4, 0) + spread(d[248:256])[1]
        return jnp.concatenate([body, last], axis=0)

    for side, ro, row in ((0, 0, 1), (1, 2, R)):
        rows = jnp.concatenate([gp[0, row], gp[1, row]], axis=1)
        d = dot(wt[:, ro * H:(ro + 1) * H], rows)
        for m in range(2):
            edge = jnp.concatenate([fold(d[:, m * C:(m + 1) * C]), jnp.zeros((VP - VQ, C), F32)], axis=0)
            hsb[side, m] = edge.astype(BF16)

    def out_halo(side):
        to = band - 1 if side == 0 else band + 1
        return remote(hsb.at[side], hrb.at[1 - side], o_send.at[side], o_recv.at[1 - side], band=to)

    pl.when(band > 0)(lambda: out_halo(0).start())
    pl.when(band < NB - 1)(lambda: out_halo(1).start())

    def input_grad(m, low, high):
        def step(rp, _):
            i = rp * 2
            rows = jnp.concatenate([pair(gp, m, i + 2 - ro) for ro in range(3)], axis=0)
            d = dot(wt[...], rows)
            for k in range(2):
                value = fold(d[:, k * C:(k + 1) * C]) + gn[m, i + k].astype(F32)[0:VQ]
                of[m, pl.ds(i + k, VQ, stride=R), :] = value
            return 0

        lax.fori_loop(low, high, step, 0)

    sum_send()
    input_grad(0, 0, 8)
    input_grad(1, 0, 8)

    def out_halo_in(side, row):
        remote(hsb.at[1 - side], hrb.at[side], o_send.at[1 - side], o_recv.at[side], band=band).wait_recv()
        for m in range(2):
            of[m, pl.ds(row, VQ, stride=R), :] += hrb[side, m].astype(F32)[0:VQ]

    pl.when(band > 0)(lambda: out_halo_in(0, 0))
    pl.when(band < NB - 1)(lambda: out_halo_in(1, R - 1))

    def write(c, _):
        for m in range(2):
            value = of[m, pl.ds(pl.multiple_of(c * 192, 192), 192), :]
            out[m, pl.ds(c * 12, 12)] = value.reshape(12, R, C).astype(BF16)
        return 0

    lax.fori_loop(0, V // 12, write, 0)

    def sum_take(step, total):
        source = lax.rem(spot + GROUP - step, GROUP)
        sum_copy(source, source).wait_recv()
        return total + r3[source].astype(F32)

    total = lax.fori_loop(1, GROUP, sum_take, s3[spot].astype(F32))
    sums[...] = total * (1.0 / (MEMBERS * NB * R * C) ** 0.5)

    pl.when(band > 0)(lambda: halo(0).wait_send())
    pl.when(band < NB - 1)(lambda: halo(1).wait_send())
    for q in range(3):
        core_copy(q).wait_send()

    def sums_sent(step, _):
        sum_copy(lax.rem(spot + step, GROUP), spot).wait_send()
        return 0

    lax.fori_loop(1, GROUP, sums_sent, 0)
    pl.when(band > 0)(lambda: out_halo(0).wait_send())
    pl.when(band < NB - 1)(lambda: out_halo(1).wait_send())

    def sent(step, _):
        j = lax.rem(me + step, NM)
        for pr in range(2):
            predicted_copy(pr, j, me).wait_send()
            gradient_copy(pr, j, me).wait_send()
        return 0

    lax.fori_loop(1, NM, sent, 0)


def finish(grads, sums, out, conv, proj):
    out[...] = grads[...]
    wide = jnp.concatenate([sums[k * 4:(k + 1) * 4, :] for k in range(7)], axis=1)
    parts = []
    for base in (0, 384, 640):
        for co in range(3):
            parts += [wide[:, base + co * 80:base + (co + 1) * 80], wide[:, base + 240 + co * 4:base + 244 + co * 4]]
    conv[...] = jnp.concatenate(parts, axis=1)
    proj[...] = wide[:, KP:KP + V]


def on_device(states, noise_field, target, w_conv, w_proj, matchings):
    vmem = pl.BlockSpec(memory_space=pltpu.VMEM)
    smem = pl.BlockSpec(memory_space=pltpu.SMEM)
    D = pltpu.SemaphoreType.DMA
    S = pltpu.VMEM
    hbm = pl.BlockSpec(memory_space=pl.ANY)
    scratch = [
        S(states.shape, BF16), S(noise_field.shape, F32), S(target.shape, BF16), S((9 * V, H), BF16), S((V, H), BF16),
        S((8, 8 * C, C), BF16), S((MEMBERS, C), jnp.int32), pltpu.SMEM((MEMBERS, C), jnp.int32), S((9 * V, H), F32), D((7,)),
        S((2, VP * R, C), F32), S((2, R + 2, KP, C), BF16), S((2, 2, VP, C), BF16), S((2, 2, VP, C), BF16),
        S((H, 3 * KP), BF16), S((KP, 3 * H), BF16), S((VP, H), BF16), S((H, VP), BF16),
        S((2, R, H, C), BF16), S((2, R, H, C), F32), S((4, 2 * VP, 2 * C), BF16),
        S((2, NM, 2, VH, C), BF16), S((2, NM, 2, VH, C), BF16), S((MEMBERS, VH, C), F32),
        S((VP * R, C), F32), S((2, VH, C), F32), S(((NK + 1) * MEMBERS * 8, C), F32), S(((NK + 1) * MEMBERS, C), F32),
        S((2, NM, 2, VH, C), BF16), S((2, NM, 2, VH, C), BF16), S((2, R, VP, C), BF16),
        S((2, R + 2, H, C), BF16), S((2, VP * R, C), F32),
        S((2, 2, VP, C), BF16), S((2, 2, VP, C), BF16),
        *[S((H, w), F32) for w in CHUNKS],
        *[S((8, 32, w), BF16) for _ in range(2) for w in CHUNKS],
        S((GROUP, 32, C), BF16), S((GROUP, 32, C), BF16),
        D((2,)), D((2,)), D((2, NM)), D((2, NM)), D((2, NM)), D((2, NM)), D((2,)), D((2,)),
        D((3,)), D((3,)), D((GROUP,)), D((GROUP,)), pltpu.SemaphoreType.REGULAR,
    ]
    grad_states, sums = pl.pallas_call(
        kernel,
        out_shape=(
            jax.ShapeDtypeStruct(states.shape, BF16),
            jax.ShapeDtypeStruct((32, C), F32),
        ),
        in_specs=[hbm] * 6 + [smem, vmem],
        out_specs=(vmem, vmem),
        scratch_shapes=scratch,
        compiler_params=pltpu.CompilerParams(
            collective_id=0, has_side_effects=True, vmem_limit_bytes=60 * 1024 * 1024
        ),
    )(
        states, noise_field, target, w_conv.T, w_proj, jnp.asarray(patch_order()), matchings, matchings,
    )
    grad_states, grad_conv, grad_proj = pl.pallas_call(
        finish,
        out_shape=(
            jax.ShapeDtypeStruct(states.shape, BF16),
            jax.ShapeDtypeStruct((4, 9 * V), F32),
            jax.ShapeDtypeStruct((4, V), F32),
        ),
        in_specs=[vmem] * 2,
        out_specs=(vmem,) * 3,
    )(grad_states, sums)
    return grad_states, grad_conv, grad_proj.T


def solution(mesh):
    return jax.shard_map(
        on_device,
        mesh=mesh,
        in_specs=(
            P("member", None, "band", None),
            P("member", None, "band", None),
            P(None, "band", None),
            P(),
            P(),
            P(),
        ),
        out_specs=(
            P("member", None, "band", None),
            P(("member", "band"), None),
            P(None, ("member", "band")),
        ),
        check_vma=False,
    )
```

profile of v0, /device:TPU:1, one launch (start us, length us, event | category | flops | bytes accessed | tf_op | source)
XLA Modules:
  0.0 60.1 jit_solution(6271902038706999390)
XLA Ops:
  0.6 57.4 %shard_map.94 = (bf16[2,84,16,128]{3,2,1,0:T(8,128)(2,1)}, f32[32,128]{1,0:T(8,128)}) custom-call(bf16[2,84,16,128]{3,2,1,0:T(8,128)(2,1)} %states_in.1, f32[2,84,16,128]{3,2,1,0:T(8,128)} %noise_in.1, bf16[84,16,128]{2,1,0:T(8,128)(2,1)} %target_in.1, bf16[756,512]{1,0:T(8,128)(2,1)} %bitcast.2, bf16[84,512]{1,0:T(8,128)(2,1)} %w_proj_in.1, ...), custom_call_target="tpu_custom_call" | custom-call | tf_op jit(solution)/shard_map/pallas_call | solution.py:543
  58.1 2.0 %shard_map.95 = (bf16[2,84,16,128]{3,2,1,0:T(8,128)(2,1)}, f32[4,756]{1,0:T(4,128)}, f32[4,84]{1,0:T(4,128)}) custom-call(bf16[2,84,16,128]{3,2,1,0:T(8,128)(2,1)} %get-tuple-element.8.grads, f32[32,128]{1,0:T(8,128)} %get-tuple-element.9.sums), custom_call_target="tpu_custom_call" | custom-call | tf_op jit(solution)/shard_map/pallas_call | solution.py:558
where the time goes:
time: 60.4 us; the launch traced here: 60.1 us
  Pallas kernels  59.4 us (98%)
  between operations  0.64 us (1%)
    pallas_call x1, Pallas kernels, on_device(): pl.pallas_call(kernel, out_shape=(jax.ShapeDtypeStruct(states.shape, BF16...  57.4 us
    pallas_call x1, Pallas kernels, on_device(): pl.pallas_call(finish, out_shape=(jax.ShapeDtypeStruct(states.shape, BF16...  2 us

commit v1 on v0

--- a/solution.py
+++ b/solution.py
@@ -37,10 +37,13 @@
     )
 
 
-def gelu_and_slope(x):
-    phi = 0.5 + 0.5 * lax.erf(x * 0.7071067811865476)
+def gelu(x):
+    return x * (0.5 + 0.5 * lax.erf(x * 0.7071067811865476))
+
+
+def gelu_slope(x):
     bell = jnp.exp2((x * x) * (-0.5 * 1.4426950408889634) - 1.3257480647361593)
-    return x * phi, phi + x * bell
+    return 0.5 + 0.5 * lax.erf(x * 0.7071067811865476) + x * bell
 
 
 def dot(a, b):
@@ -199,12 +202,20 @@
             columns = jnp.concatenate([pair(x3, m, i + ro) for ro in range(3)], axis=0)
             for part in range(0, H, H // 2):
                 rows = slice(part, part + H // 2)
-                value, grad = gelu_and_slope(dot(wf[rows, :], columns))
-                value = value.astype(BF16)
+                pre = dot(wf[rows, :], columns)
+                value = gelu(pre).astype(BF16)
                 for k in range(2):
                     hidden[m, i + k, rows, :] = value[:, k * C:(k + 1) * C]
-                    slope[m, i + k, rows, :] = grad[:, k * C:(k + 1) * C]
-        return 0
+                    slope[m, i + k, rows, :] = pre[:, k * C:(k + 1) * C]
+        return 0
+
+    def slopes(pr):
+        def step(r, _):
+            for m in range(2):
+                slope[m, pr * 8 + r] = gelu_slope(slope[m, pr * 8 + r])
+            return 0
+
+        lax.fori_loop(0, 8, step, 0)
 
     def predict(pr):
         for m in range(2):
@@ -392,20 +403,22 @@
         lax.fori_loop(1, GROUP, send, 0)
 
     lax.fori_loop(1, 4, forward, 0)
+    halo_rows()
+    forward(0, 0)
+    predict(0)
+    lax.fori_loop(4, 8, forward, 0)
+    predict(1)
     truth_patches()
     gp_zero = jnp.zeros((H, C), BF16)
     for m in range(2):
         gp[m, 0] = gp_zero
         gp[m, R + 1] = gp_zero
     acc[0][:, KP:] = jnp.zeros((H, 128), F32)
-    halo_rows()
-    forward(0, 0)
-    predict(0)
-    lax.fori_loop(4, 8, forward, 0)
-    predict(1)
     to_scalars.wait()
     score(0)
+    slopes(0)
     score(1)
+    slopes(1)
     back_to_rows(0)
     proj_term(0)
     for ro in range(3):

time: 60.4 us -> 59.4 us (0.983)
  Pallas kernels: 59.4 us -> 58.6 us
    pallas_call x1, Pallas kernels: 57.4 us -> 56.6 us  [on_device(): pl.pallas_call(kernel, out_shape=(jax.ShapeDtypeStruct(states.shape, BF16...]
where the time goes in v1:
time: 59.4 us; the launch traced here: 59.2 us
  Pallas kernels  58.6 us (99%)
  between operations  0.64 us (1%)
    pallas_call x1, Pallas kernels, on_device(): pl.pallas_call(kernel, out_shape=(jax.ShapeDtypeStruct(states.shape, BF16...  56.6 us
    pallas_call x1, Pallas kernels, on_device(): pl.pallas_call(finish, out_shape=(jax.ShapeDtypeStruct(states.shape, BF16...  2 us

profile of v1, /device:TPU:1, one launch (start us, length us, event | category | flops | bytes accessed | tf_op | source)
XLA Modules:
  0.0 59.2 jit_solution(8294426040771488627)
XLA Ops:
  0.6 56.6 %shard_map.94 = (bf16[2,84,16,128]{3,2,1,0:T(8,128)(2,1)}, f32[32,128]{1,0:T(8,128)}) custom-call(bf16[2,84,16,128]{3,2,1,0:T(8,128)(2,1)} %states_in.1, f32[2,84,16,128]{3,2,1,0:T(8,128)} %noise_in.1, bf16[84,16,128]{2,1,0:T(8,128)(2,1)} %target_in.1, bf16[756,512]{1,0:T(8,128)(2,1)} %bitcast.2, bf16[84,512]{1,0:T(8,128)(2,1)} %w_proj_in.1, ...), custom_call_target="tpu_custom_call" | custom-call | tf_op jit(solution)/shard_map/pallas_call | solution.py:556
  57.2 2.0 %shard_map.95 = (bf16[2,84,16,128]{3,2,1,0:T(8,128)(2,1)}, f32[4,756]{1,0:T(4,128)}, f32[4,84]{1,0:T(4,128)}) custom-call(bf16[2,84,16,128]{3,2,1,0:T(8,128)(2,1)} %get-tuple-element.8.grads, f32[32,128]{1,0:T(8,128)} %get-tuple-element.9.sums), custom_call_target="tpu_custom_call" | custom-call | tf_op jit(solution)/shard_map/pallas_call | solution.py:571
